TPU v7x, 256 devices: a whole 4x4x8 slice. The times are simulated.
256 devices in a mesh: row: 16 (over z_lo, x, core), col: 16 (over z_hi, y).
Axes of the slice: x: 4, y: 4, z: 8 (z_hi: 4, z_lo: 2; z = z_hi * 2 + z_lo), core: 2. Of those that a mesh axis runs over, the one named last changes fastest.
Arguments:
- activations: bfloat16 [1152, 28672], P('row', 'col'), may hold values from -6 to 6
- grad_outputs: bfloat16 [1152, 8192], P('col', 'row'), may hold values from -6 to 6
- input_basis: bfloat16 [28672, 28672], P('col', 'row'), may hold values from -0.03125 to 0.03125
- output_basis: bfloat16 [8192, 8192], P('row', 'col'), may hold values from -0.0625 to 0.0625
- segment_ids: int32 [1152], replicated, may hold values from 0 to 2, never falling along the last dimension, each value on 1 to 576 neighbouring positions
Outputs:
- correction: float32 [28672, 8192], P('row', 'col')
Inputs may be any that keep to these rules, and one draw needn't show every extreme that they name: `segment_ids`: segment ids never fall along the tokens; each of the 3 sequences has 1 to 576 tokens, one exactly 576.
All inputs are finite; a program needn't handle non-finite values.
Results may differ from a plain program's by a relative error of at most 0.0037.
Values may be sent and summed in bfloat16 or wider, within the bound.
A program may use at most 64 MiB of HBM per device.

v0:
```python
import jax
import jax.numpy as jnp
from jax import lax
from jax.sharding import PartitionSpec as P

NSEQ = 3
SEQ_MOST = 576


def shards(activations, grad_outputs, input_basis, output_basis, segment_ids):
    act_all = lax.all_gather(activations, "row", axis=0, tiled=True)
    grad_all = lax.all_gather(grad_outputs, "col", axis=0, tiled=True)
    grad_part = jnp.dot(grad_all, output_basis, preferred_element_type=jnp.float32)
    grad_rot = lax.psum(grad_part, "row").astype(jnp.bfloat16)
    labels = jnp.arange(NSEQ, dtype=jnp.int32)
    onehot = segment_ids[None, :] == labels[:, None]
    counts = jnp.sum(onehot.astype(jnp.float32), axis=1)
    weights = 1.0 / (counts * NSEQ)
    total_tokens = segment_ids.shape[0]
    span = SEQ_MOST
    count_ints = jnp.sum(onehot.astype(jnp.int32), axis=1)
    starts = jnp.cumsum(count_ints) - count_ints
    window_starts = jnp.minimum(starts, total_tokens - span)
    grad_windows = []
    for index in range(NSEQ):
        grad_window = lax.dynamic_slice_in_dim(grad_rot, window_starts[index], span, 0)
        window_ids = lax.dynamic_slice_in_dim(segment_ids, window_starts[index], span, 0)
        member = (window_ids == index).astype(jnp.bfloat16)
        grad_windows.append(grad_window * member[:, None])
    rotated = lax.psum_scatter(
        lax.dot_general(
            input_basis, act_all, (((0,), (1,)), ((), ())), preferred_element_type=jnp.float32
        ),
        "col",
        scatter_dimension=0,
        tiled=True,
    ).astype(jnp.bfloat16)
    shard_piece = lax.all_gather(rotated, "col", axis=0, tiled=True)
    total = jnp.zeros((shard_piece.shape[0], grad_rot.shape[1]), jnp.float32)
    for index in range(NSEQ):
        act_window = lax.dynamic_slice_in_dim(shard_piece, window_starts[index], span, 1)
        per_sequence = jnp.dot(act_window, grad_windows[index], preferred_element_type=jnp.float32)
        total = total + per_sequence * per_sequence * weights[index]
    return total


def solution(mesh):
    placed = (P("row", "col"), P("col", "row"), P("col", "row"), P("row", "col"), P())
    return jax.shard_map(
        shards, mesh=mesh, in_specs=placed, out_specs=P("row", "col"), check_vma=False
    )
```

profile of v0, /device:TPU:1, one launch (start us, length us, event | category | flops | bytes accessed | tf_op | source)
XLA Modules:
  0.0 354.8 jit_solution(16610075228979062483)
XLA Ops:
  6.5 0.0 copy-start
  6.5 0.0 all-gather.4.cloned.1.call-start
  6.5 0.7 all-gather.4.cloned.1.call-update
  7.3 0.0 reduce-scatter.2.cloned.1.call-start
  7.3 46.0 %all-gather.4.cloned.1.call-done = bf16[1152,1792]{1,0:T(8,128)(2,1)} async-done(((bf16[72,1792]{1,0:T(8,128)(2,1)}), bf16[1152,1792]{1,0:T(8,128)(2,1)}) %all-gather.4.cloned.1.call-update) | async-done | bytes 4128784 | tf_op jit(solution)/shard_map/all_gather | solution.py:11
  53.3 13.8 %fusion.21 = f32[1792,1152]{1,0:T(8,128)} fusion(bf16[1792,1792]{1,0:T(8,128)(2,1)} %param.7, bf16[1152,1792]{1,0:T(8,128)(2,1)} %all-gather.4.cloned.1.call-done), kind=kOutput, calls=%fused_computation.33 | convolution fusion | flops 7398752256 | bytes 18808832 | tf_op jit(solution)/shard_map/dot_general | solution.py:31
  67.1 0.0 copy-start.3
  67.1 0.0 reduce-scatter.2.cloned.1.call-update
  67.1 0.0 all-gather.8.cloned.1.call-start
  67.2 0.7 all-gather.8.cloned.1.call-update
  67.9 0.0 all-gather.6.cloned.1.call-start
  67.9 118.4 %reduce-scatter.2.cloned.1.call-done = f32[112,1152]{1,0:T(8,128)} async-done(((f32[1792,1152]{1,0:T(8,128)}), f32[112,1152]{1,0:T(8,128)}) %reduce-scatter.2.cloned.1.call-update) | async-done | bytes 516112 | tf_op jit(solution)/shard_map/reduce_scatter | solution.py:30
  186.3 1.8 convert_element_type.21
  188.1 0.0 all-gather.6.cloned.1.call-update
  188.1 0.0 copy-done.3
  188.1 0.1 convert_reduce_fusion.1
  188.2 0.2 reduce-window.9
  188.4 0.7 fusion.20
  195.0 0.1 fusion.12
  195.1 0.1 convert_reduce_fusion
  195.2 0.6 fusion.19
  195.8 46.2 %all-gather.8.cloned.1.call-done = bf16[1152,512]{1,0:T(8,128)(2,1)} async-done(((bf16[72,512]{1,0:T(8,128)(2,1)}), bf16[1152,512]{1,0:T(8,128)(2,1)}) %all-gather.8.cloned.1.call-update) | async-done | bytes 1179664 | tf_op jit(solution)/shard_map/all_gather | solution.py:12
  242.1 0.0 copy-done
  242.1 2.1 fusion.22
  244.1 92.7 %all-reduce.1 = bf16[1152,512]{1,0:T(8,128)(2,1)} all-reduce(f32[1152,512]{1,0:T(8,128)S(1)} %fusion.22), channel_id=1, replica_groups=mesh['row'=16,'col'=16] {'row'}, use_global_device_ids=true, to_apply=%region_3.0 | all-reduce | flops 589824 | bytes 3538944 | tf_op jit(solution)/shard_map/psum | solution.py:14
  336.8 0.0 all-gather.6.cloned.1.call-done
  336.8 0.0 copy-start.1
  336.8 0.0 copy-start.2
  336.8 3.7 %convolution_multiply_fusion.1 = f32[1792,512]{1,0:T(8,128)S(1)} fusion(bf16[1792,1152]{1,0:T(8,128)(2,1)} %all-gather.6.cloned.1.call-done, s32[]{:T(128)S(6)} %select_n.7, bf16[1152,512]{1,0:T(8,128)(2,1)} %all-reduce.1, bf16[576]{0:T(1024)(128)(2,1)S(1)} %get-tuple-element.7), kind=kOutput, calls=%fused_computation.1 | convolution fusion | flops 1059061760 | bytes 6555776 | tf_op jit(solution)/shard_map/dot_general | solution.py:42
  340.5 0.0 copy-done.1
  340.5 0.0 copy-done.2
  340.5 1.8 convolution_multiply_fusion
  342.3 6.0 %multiply_add_fusion = f32[1792,512]{1,0:T(8,128)} fusion(f32[1792,512]{1,0:T(8,128)S(1)} %convolution_multiply_fusion, f32[1792,512]{1,0:T(8,128)S(1)} %convolution_multiply_fusion.1, bf16[1792,1152]{1,0:T(8,128)(2,1)S(1)} %copy-done.2, s32[]{:T(128)S(6)} %select_n.6, f32[]{:T(128)} %bitcast.7, f32[]{:T(128)} %bitcast.5, f32[]{:T(128)} %bitcast.3, ...), kind=kOutput, calls=%fused_computation.3 | convolution fusion | flops 1063649280 | bytes 13896716 | tf_op jit(solution)/shard_map/dot_general | solution.py:42
  (2 shorter events, 0.0 us)
Async XLA Ops:
  6.5 235.5 %copy-start = (bf16[512,512]{1,0:T(8,128)(2,1)S(1)}, bf16[512,512]{1,0:T(8,128)(2,1)}, u32[]{:S(2)}) copy-start(bf16[512,512]{1,0:T(8,128)(2,1)} %param.8) | copy-start | bytes 1572868
  6.5 46.7 %all-gather.4.cloned.1.call-start = ((), (), s32[]{:S(2)}) async-start(), calls=%async_computation.1 | async-start | bytes 4386816 | tf_op jit(solution)/shard_map/all_gather | solution.py:11
  7.3 179.1 %reduce-scatter.2.cloned.1.call-start = ((), (), s32[]{:S(2)}) async-start(), calls=%async_computation.2 | async-start | bytes 8773632 | tf_op jit(solution)/shard_map/reduce_scatter | solution.py:30
  67.1 121.0 %copy-start.3 = (s32[1152]{0:T(1024)S(1)}, s32[1152]{0:T(1024)}, u32[]{:S(2)}) copy-start(s32[1152]{0:T(1024)} %param.9) | copy-start | bytes 13828
  67.1 174.9 %all-gather.8.cloned.1.call-start = ((), (), s32[]{:S(2)}) async-start(), calls=%async_computation.4 | async-start | bytes 1253376 | tf_op jit(solution)/shard_map/all_gather | solution.py:12
  67.9 268.9 %all-gather.6.cloned.1.call-start = ((), (), s32[]{:S(2)}) async-start(), calls=%async_computation.3 | async-start | bytes 4386816 | tf_op jit(solution)/shard_map/all_gather | solution.py:38
  336.8 3.7 %copy-start.1 = (bf16[1152,512]{1,0:T(8,128)(2,1)S(1)}, bf16[1152,512]{1,0:T(8,128)(2,1)}, u32[]{:S(2)}) copy-start(bf16[1152,512]{1,0:T(8,128)(2,1)} %all-reduce.1) | copy-start | bytes 3538948
  336.8 3.7 %copy-start.2 = (bf16[1792,1152]{1,0:T(8,128)(2,1)S(1)}, bf16[1792,1152]{1,0:T(8,128)(2,1)}, u32[]{:S(2)}) copy-start(bf16[1792,1152]{1,0:T(8,128)(2,1)} %all-gather.6.cloned.1.call-done) | copy-start | bytes 12386308
Sparse Core Ops, SparseCore 0:
  9.2 44.0 all-gather.3
  67.2 119.0 reduce-scatter.1
  188.8 53.2 all-gather.7
  244.4 82.8 all-gather.5
where the time goes:
time: 357 us; the launch traced here: 355 us
  waiting for transfers between devices  212 us (59%)
  blocking collectives  92.7 us (26%)
  matrix products  27.3 us (8%)
  between operations  19.1 us (5%)
    reduce_scatter x1, waiting for transfers between devices, shards(): lax.psum_scatter(lax.dot_general(input_basis, act_all, (((0,), (1,)), (()...  118 us
    psum x1, blocking collectives, shards(): grad_rot = lax.psum(grad_part, 'row').astype(jnp.bfloat16)  92.7 us
    all_gather x1, waiting for transfers between devices, shards(): grad_all = lax.all_gather(grad_outputs, 'col', axis=0, tiled=True)  46.2 us
    all_gather x1, waiting for transfers between devices, shards(): act_all = lax.all_gather(activations, 'row', axis=0, tiled=True)  46 us
    dot_general x1, matrix products, shards(): lax.dot_general(input_basis, act_all, (((0,), (1,)), ((), ())), preferred...  13.8 us
    dot_general x3, matrix products, shards(): jnp.dot(act_window, grad_windows[index], preferred_element_type=jnp.float32)  11.4 us
  transfers between devices with their start and end apart: 4, of which 3 were waited for; matrix products, arithmetic and copies ran while one was open for 2% of the time, Pallas kernels for 0%

commit v1 on v0

v1 whole, which is shorter than its diff:
```python
import jax
import jax.numpy as jnp
from jax import lax
from jax.experimental import pallas as pl
from jax.experimental.pallas import tpu as pltpu
from jax.sharding import PartitionSpec as P

MESH = pl.DeviceIdType.MESH
NSEQ = 3
TOK = 1152
SLAB = 72
CIN = 1792
GIN = 512
STEPS = 7
WIDE = 256
QUARTER = 64
HALF = 32
PIECE = 16
TILE = 384
BF = jnp.bfloat16
F32 = jnp.float32


def kernel(
    act, grad, basis, obasis, ids, out,
    slabs, acts, bas, obas, part, half_out, half_in, full_out, full_in, z_out, z_in, rot, res,
    gslabs, gpart, gcore, gin, grot,
    send, recv, asend, arecv, gsend, grecv, local,
):
    r, c = lax.axis_index("row"), lax.axis_index("col")
    core, x, zl = r % 2, (r // 2) % 4, r // 8
    y, zh = c % 4, c // 4
    chip = zl * 4 + x

    def row_dev(x_, zl_, core_):
        return {"row": zl_ * 8 + x_ * 2 + core_, "col": c}

    def col_dev(y_, zh_):
        return {"row": r, "col": zh_ * 4 + y_}

    twin = row_dev(x, zl, 1 - core)
    x_up, x_dn = row_dev((x + 1) % 4, zl, core), row_dev((x + 3) % 4, zl, core)
    z_pair = row_dev(x, 1 - zl, core)
    y_up, y_dn = col_dev((y + 1) % 4, zh), col_dev((y + 3) % 4, zh)

    def chip_dev(k):
        return {"row": k * 2 + core, "col": c}

    barrier = pltpu.get_barrier_semaphore()
    for dev in [twin, y_up, y_dn] + [col_dev(y, (zh + o) % 4) for o in (1, 2, 3)] + [
        chip_dev((chip + o) % 8) for o in range(1, 8)
    ]:
        pl.semaphore_signal(barrier, inc=1, device_id=dev, device_id_type=MESH)
    pl.semaphore_wait(barrier, 13)

    def remote(src, dst, s, d, dev):
        return pltpu.make_async_remote_copy(
            src_ref=src, dst_ref=dst, send_sem=s, recv_sem=d, device_id=dev, device_id_type=MESH
        )

    own_act = pltpu.make_async_copy(act, slabs.at[r], local.at[0])
    own_grad = pltpu.make_async_copy(grad, gslabs.at[c], local.at[1])
    own_act.start()
    own_grad.start()
    own_ob = pltpu.make_async_copy(obasis, obas, local.at[2])
    own_ob.start()

    def basis_copy(j):
        return pltpu.make_async_copy(
            basis.at[:, pl.ds(pl.multiple_of(j * WIDE, WIDE), WIDE)], bas.at[j], local.at[3 + j]
        )

    def slab_at(x_, zl_, core_):
        return slabs.at[zl_ * 8 + x_ * 2 + core_]

    LO, HI = slice(0, CIN // 2), slice(CIN // 2, CIN)

    def ship(n, src, dst, dev):
        d = remote(src, dst, asend.at[n], arecv.at[n], dev)
        d.start()

    def landed(n, dst, dev):
        remote(dst, dst, asend.at[n], arecv.at[n], dev).wait_recv()

    xm, xp, xo, zo = (x + 3) % 4, (x + 1) % 4, (x + 2) % 4, 1 - zl
    mine = slabs.at[r]

    ship(0, act, mine, z_pair)
    ship(1, act, mine, x_up)
    ship(2, act, mine, x_dn)
    ship(9, act, mine, twin)

    def gship(n, src, dst, dev):
        remote(src, dst, gsend.at[n], grecv.at[n], dev).start()

    def glanded(n, dst, dev):
        remote(dst, dst, gsend.at[n], grecv.at[n], dev).wait_recv()

    for o in (1, 2, 3):
        h = (zh + o) % 4
        remote(grad, gslabs.at[c], gsend.at[h], grecv.at[zh], col_dev(y, h)).start()

    for j in range(STEPS):
        basis_copy(j).start()

    landed(0, slab_at(x, zo, core), z_pair)
    ship(3, slab_at(x, zo, core), slab_at(x, zo, core), x_up)
    ship(4, slab_at(x, zo, core), slab_at(x, zo, core), x_dn)
    ship(10, slab_at(x, zo, core), slab_at(x, zo, core), twin)

    own_grad.wait()
    for o in (1, 2, 3):
        h = (zh + o) % 4
        glanded(h, gslabs.at[h * 4 + y], col_dev(y, h))
    for h in range(4):
        piece = gslabs.at[h * 4 + y]
        gship(4 + h, piece, piece, y_up)
        gship(8 + h, piece, piece, y_dn)

    def relay(n_up, n_dn, n_half_up, n_half_dn, n_twin_m, n_twin_p, zl_):
        below, above = slab_at(xm, zl_, core), slab_at(xp, zl_, core)
        landed(n_up, below, x_dn)
        ship(n_half_up, below.at[:, LO], below.at[:, LO], x_up)
        ship(n_twin_m, below, below, twin)
        landed(n_dn, above, x_up)
        ship(n_half_dn, above.at[:, HI], above.at[:, HI], x_dn)
        ship(n_twin_p, above, above, twin)

    relay(1, 2, 5, 6, 11, 12, zl)

    for h in range(4):
        glanded(4 + h, gslabs.at[h * 4 + (y + 3) % 4], y_dn)
        glanded(8 + h, gslabs.at[h * 4 + (y + 1) % 4], y_up)
    for h in range(2):
        piece = gslabs.at[h * 4 + (y + 3) % 4]
        gship(12 + h, piece, piece, y_up)
        piece = gslabs.at[(2 + h) * 4 + (y + 1) % 4]
        gship(14 + h, piece, piece, y_dn)

    relay(3, 4, 7, 8, 13, 14, zo)

    for n, zl_ in ((5, zl), (7, zo)):
        far = slab_at(xo, zl_, core)
        landed(n, far.at[:, LO], x_dn)
        landed(n + 1, far.at[:, HI], x_up)
        ship(15 if n == 5 else 16, far, far, twin)

    for h in range(2):
        glanded(12 + h, gslabs.at[h * 4 + (y + 2) % 4], y_dn)
        glanded(14 + h, gslabs.at[(2 + h) * 4 + (y + 2) % 4], y_up)
    own_ob.wait()

    def rotate_grad(k, carry):
        a = gslabs[2 * k].astype(F32)
        b = gslabs[2 * k + 1].astype(F32)
        both = jnp.concatenate([a, b], axis=0).astype(BF)
        prod = jnp.dot(both, obas[...], preferred_element_type=F32)
        gpart[0, k] = prod[:, :256]
        gpart[1, k] = prod[:, 256:]
        return carry

    lax.fori_loop(0, 8, rotate_grad, 0)
    gship(16, gpart.at[1 - core], gcore, twin)

    own_act.wait()
    for n, x_, zl_ in (
        (9, x, zl), (10, x, zo), (11, xm, zl), (12, xp, zl), (13, xm, zo), (14, xp, zo), (15, xo, zl), (16, xo, zo),
    ):
        landed(n, slab_at(x_, zl_, 1 - core), twin)

    def join(k, carry):
        a = slabs[2 * k].astype(F32)
        b = slabs[2 * k + 1].astype(F32)
        acts[pl.ds(pl.multiple_of(k * 144, 16), 144), :] = jnp.concatenate([a, b], axis=0).astype(BF)
        return carry

    lax.fori_loop(0, 8, join, 0)

    label = ids[...]
    members = [(label == s) for s in range(NSEQ)]
    weights = [1.0 / (jnp.sum(m.astype(F32), axis=1, keepdims=True) * NSEQ) for m in members]
    masks = [m.astype(F32).astype(BF) for m in members]

    def msg(j, n_send, n_recv, src, dst, dev):
        return remote(src, dst, send.at[j, n_send], recv.at[j, n_recv], dev)

    def stage_compute(j):
        basis_copy(j).wait()

        def tile(m, carry):
            at = pl.multiple_of(m * TILE, TILE)
            prod = jnp.dot(acts[pl.ds(at, TILE), :], bas[j], preferred_element_type=F32)
            part[j, :, :, pl.ds(at, TILE)] = prod.T.reshape(4, QUARTER, TILE)
            return carry

        lax.fori_loop(0, TOK // TILE, tile, 0)
        d = (y + 2) % 4
        half_out[j, 0] = part[j, d, :HALF].astype(BF)
        half_out[j, 1] = part[j, d, HALF:].astype(BF)
        msg(j, 0, 0, half_out.at[j, 0], half_in.at[j, 0], y_up).start()
        msg(j, 1, 1, half_out.at[j, 1], half_in.at[j, 1], y_dn).start()

    def stage_half(j):
        up, dn = (y + 1) % 4, (y + 3) % 4
        msg(j, 0, 0, half_out.at[j, 0], half_in.at[j, 0], y_dn).wait_recv()
        full_out[j, 0, :HALF] = (part[j, up, :HALF] + half_in[j, 0].astype(F32)).astype(BF)
        full_out[j, 0, HALF:] = part[j, up, HALF:].astype(BF)
        msg(j, 2, 2, full_out.at[j, 0], full_in.at[j, 0], y_up).start()
        msg(j, 1, 1, half_out.at[j, 1], half_in.at[j, 1], y_up).wait_recv()
        full_out[j, 1, HALF:] = (part[j, dn, HALF:] + half_in[j, 1].astype(F32)).astype(BF)
        full_out[j, 1, :HALF] = part[j, dn, :HALF].astype(BF)
        msg(j, 3, 3, full_out.at[j, 1], full_in.at[j, 1], y_dn).start()

    def stage_full(j):
        msg(j, 2, 2, full_out.at[j, 0], full_in.at[j, 0], y_dn).wait_recv()
        msg(j, 3, 3, full_out.at[j, 1], full_in.at[j, 1], y_up).wait_recv()
        total = part[j, y] + full_in[j, 0].astype(F32) + full_in[j, 1].astype(F32)
        part[j, y] = total
        z_out[j] = total.astype(BF).reshape(4, PIECE, TOK)
        for o in (1, 2, 3):
            h = (zh + o) % 4
            msg(j, 4 + h, 4 + zh, z_out.at[j, h], z_in.at[j, zh], col_dev(y, h)).start()

    def stage_z(j):
        total = part[j, y, pl.ds(pl.multiple_of(zh * PIECE, PIECE), PIECE), :]
        for o in (1, 2, 3):
            h = (zh + o) % 4
            msg(j, 4 + h, 4 + h, z_out.at[j, h], z_in.at[j, h], col_dev(y, h)).wait_recv()
            total = total + z_in[j, h].astype(F32)
        rot[j, y, zh] = total.astype(BF)
        for o in (1, 2, 3):
            h = (zh + o) % 4
            piece = rot.at[j, y, zh]
            msg(j, 8 + h, 8 + zh, piece, piece, col_dev(y, h)).start()

    def stage_gather(j):
        for o in (1, 2, 3):
            h = (zh + o) % 4
            piece = rot.at[j, y, h]
            msg(j, 8 + h, 8 + h, piece, piece, col_dev(y, h)).wait_recv()
        quarter = rot.at[j, y]
        msg(j, 12, 12, quarter, quarter, y_up).start()
        msg(j, 13, 13, quarter, quarter, y_dn).start()

    def stage_relay(j):
        below, above = rot.at[j, (y + 3) % 4], rot.at[j, (y + 1) % 4]
        msg(j, 12, 12, below, below, y_dn).wait_recv()
        piece = below.at[0:2]
        msg(j, 14, 14, piece, piece, y_up).start()
        msg(j, 13, 13, above, above, y_up).wait_recv()
        piece = above.at[2:4]
        msg(j, 15, 15, piece, piece, y_dn).start()

    def out_copy(j):
        return pltpu.make_async_copy(
            res.at[j], out.at[pl.ds(pl.multiple_of(j * WIDE, WIDE), WIDE), :], local.at[10 + j]
        )

    def stage_out(j):
        far = rot.at[j, (y + 2) % 4]
        msg(j, 14, 14, far.at[0:2], far.at[0:2], y_dn).wait_recv()
        msg(j, 15, 15, far.at[2:4], far.at[2:4], y_up).wait_recv()
        a = rot[j].reshape(WIDE, TOK)
        for h in range(2):
            g = grot[h].reshape(TOK, 256)
            total = None
            for s in range(NSEQ):
                p = jnp.dot(a * masks[s], g, preferred_element_type=F32)
                term = p * p * weights[s]
                total = term if total is None else total + term
            res[j, :, pl.ds(h * 256, 256)] = total
        out_copy(j).start()

    def grad_core():
        glanded(16, gcore, twin)

        def add(k, carry):
            gpart[core, k] = gpart[core, k] + gcore[k]
            return carry

        lax.fori_loop(0, 8, add, 0)
        for o in range(1, 8):
            k = (chip + o) % 8
            remote(gpart.at[core, k], gin.at[chip], gsend.at[17 + k], grecv.at[17 + chip], chip_dev(k)).start()

    def grad_sum():
        total = gpart[core, chip]
        for o in range(1, 8):
            k = (chip + o) % 8
            glanded(17 + k, gin.at[k], chip_dev(k))
            total = total + gin[k]
        grot[core, chip] = total.astype(BF)
        piece = grot.at[core, chip]
        for o in range(1, 8):
            k = (chip + o) % 8
            remote(piece, piece, gsend.at[25 + k], grecv.at[25 + chip], chip_dev(k)).start()

    def grad_gather():
        for o in range(1, 8):
            k = (chip + o) % 8
            glanded(25 + k, grot.at[core, k], chip_dev(k))
        gship(33, grot.at[core], grot.at[core], twin)

    def grad_done():
        glanded(33, grot.at[1 - core], twin)

    stages = [stage_compute, stage_half, stage_full, stage_z, stage_gather, stage_relay, stage_out]
    extras = {1: grad_core, 3: grad_sum, 5: grad_gather, 6: grad_done}

    def turn(t, carry):
        for lag, stage in enumerate(stages):
            if lag == len(stages) - 1:
                for at, extra in extras.items():
                    pl.when(t == at)(extra)

            @pl.when((t >= lag) & (t < lag + STEPS))
            def _():
                stage(t - lag)

        return carry

    lax.fori_loop(0, STEPS + len(stages) - 1, turn, 0)

    def finish(j, carry):
        out_copy(j).wait()
        for n in (0, 1):
            msg(j, n, n, half_out.at[j, n], half_in.at[j, n], y_up).wait_send()
            msg(j, 2 + n, 2 + n, full_out.at[j, n], full_in.at[j, n], y_up).wait_send()
            msg(j, 12 + n, 12 + n, rot.at[j, y], rot.at[j, y], y_up).wait_send()
            msg(j, 14 + n, 14 + n, rot.at[j, y, 0:2], rot.at[j, y, 0:2], y_up).wait_send()
        for o in (1, 2, 3):
            h = (zh + o) % 4
            for base in (4, 8):
                msg(j, base + h, base + h, rot.at[j, y, h], rot.at[j, y, h], col_dev(y, h)).wait_send()
        return carry

    lax.fori_loop(0, STEPS, finish, 0)

    def sent(sem, ref, dev):
        remote(ref, ref, sem, sem, dev).wait_send()

    for n in (0, 1, 2, 3, 4, 9, 10, 11, 12, 13, 14, 15, 16):
        sent(asend.at[n], mine, twin)
    for n in (5, 6, 7, 8):
        sent(asend.at[n], mine.at[:, LO], twin)
    for o in (1, 2, 3):
        sent(gsend.at[(zh + o) % 4], gslabs.at[c], twin)
    for n in range(4, 16):
        sent(gsend.at[n], gslabs.at[c], twin)
    sent(gsend.at[16], gcore, twin)
    for o in range(1, 8):
        k = (chip + o) % 8
        sent(gsend.at[17 + k], gin.at[k], twin)
        sent(gsend.at[25 + k], grot.at[core, k], twin)
    sent(gsend.at[33], grot.at[core], twin)


def shards(activations, grad_outputs, input_basis, output_basis, segment_ids):
    hbm = pl.BlockSpec(memory_space=pl.ANY)
    dma = pltpu.SemaphoreType.DMA
    return pl.pallas_call(
        kernel,
        out_shape=jax.ShapeDtypeStruct((CIN, GIN), F32),
        in_specs=[hbm, hbm, hbm, hbm, pl.BlockSpec(memory_space=pltpu.VMEM)],
        out_specs=hbm,
        scratch_shapes=[
            pltpu.VMEM((16, SLAB, CIN), BF),
            pltpu.VMEM((TOK, CIN), BF),
            pltpu.VMEM((STEPS, CIN, WIDE), BF),
            pltpu.VMEM((GIN, GIN), BF),
            pltpu.VMEM((STEPS, 4, QUARTER, TOK), F32),
            pltpu.VMEM((STEPS, 2, HALF, TOK), BF),
            pltpu.VMEM((STEPS, 2, HALF, TOK), BF),
            pltpu.VMEM((STEPS, 2, QUARTER, TOK), BF),
            pltpu.VMEM((STEPS, 2, QUARTER, TOK), BF),
            pltpu.VMEM((STEPS, 4, PIECE, TOK), BF),
            pltpu.VMEM((STEPS, 4, PIECE, TOK), BF),
            pltpu.VMEM((STEPS, 4, 4, PIECE, TOK), BF),
            pltpu.VMEM((STEPS, WIDE, GIN), F32),
            pltpu.VMEM((16, SLAB, GIN), BF),
            pltpu.VMEM((2, 8, 144, 256), F32),
            pltpu.VMEM((8, 144, 256), F32),
            pltpu.VMEM((8, 144, 256), F32),
            pltpu.VMEM((2, 8, 144, 256), BF),
            dma((STEPS, 16)),
            dma((STEPS, 16)),
            dma((17,)),
            dma((17,)),
            dma((34,)),
            dma((34,)),
            dma((17,)),
        ],
        compiler_params=pltpu.CompilerParams(
            collective_id=0, has_side_effects=True, vmem_limit_bytes=60 * 1024 * 1024
        ),
        cost_estimate=pl.CostEstimate(flops=15_000_000_000, bytes_accessed=16_000_000, transcendentals=0),
    )(activations, grad_outputs, input_basis, output_basis, segment_ids.reshape(1, TOK))


def solution(mesh):
    placed = (P("row", "col"), P("col", "row"), P("col", "row"), P("row", "col"), P())
    return jax.shard_map(
        shards, mesh=mesh, in_specs=placed, out_specs=P("row", "col"), check_vma=False
    )
```

time: 357 us -> 138 us (0.39)
  the two profiles are of different devices: /device:TPU:1 before, /device:TPU:2 now
where the time goes in v1:
time: 138 us; the launch traced here: 137 us
  Pallas kernels  132 us (96%)
  local copies, waits for them, and re-layouts  5.54 us (4%)
    pallas_call x1, Pallas kernels, shards(): pl.pallas_call(kernel, out_shape=jax.ShapeDtypeStruct((CIN, GIN), F32), i...  132 us
    unnamed x1, local copies, waits for them, and re-layouts  4.25 us

profile of v1, /device:TPU:2, one launch (start us, length us, event | category | flops | bytes accessed | tf_op | source)
XLA Modules:
  0.0 137.4 jit_solution(9655440356453641072)
XLA Ops:
  0.0 1.3 reshape.3.ids
  1.3 131.9 %shard_map.55 = f32[1792,512]{1,0:T(8,128)} custom-call(bf16[72,1792]{1,0:T(8,128)(2,1)} %act.1, bf16[72,512]{1,0:T(8,128)(2,1)} %grad.1, bf16[1792,1792]{1,0:T(8,128)(2,1)} %basis.1, bf16[512,512]{1,0:T(8,128)(2,1)} %obasis.1, s32[1,1152]{1,0:T(1,128)} %reshape.3.ids), custom_call_target="tpu_custom_call" | custom-call | flops 15000000512 | bytes 16000000 | tf_op jit(solution)/shard_map/pallas_call | solution.py:361
  133.2 4.2 %copy.7 = f32[1792,512]{1,0:T(8,128)} copy(f32[1792,512]{1,0:T(8,128)} %shard_map.55) | data formatting | bytes 7340032

commit v2 on v0

v2 whole, which is shorter than its diff:
```python
import jax
import jax.numpy as jnp
from jax import lax
from jax.experimental import pallas as pl
from jax.experimental.pallas import tpu as pltpu
from jax.sharding import PartitionSpec as P

MESH = pl.DeviceIdType.MESH
NSEQ = 3
TOK = 1152
SLAB = 72
CIN = 1792
GIN = 512
STEPS = 7
WIDE = 256
QUARTER = 64
HALF = 32
PIECE = 16
LANES = ((0, 512), (512, 640))
LEAD = 2
GDONE = 26
LAGS = (0, 2, 4, 7, 10, 12, 14)
BF = jnp.bfloat16
F32 = jnp.float32


def kernel(
    act, grad, basis, obasis, ids, out,
    slabs, acts, bas, obas, part, half_out, half_in, full_out, full_in, z_out, z_in, rot, res,
    gslabs, gpart, gcore, gin, gpair, grot, gmask, labels,
    send, recv, asend, arecv, gsend, grecv, local,
):
    r, c = lax.axis_index("row"), lax.axis_index("col")
    core, x, zl = r % 2, (r // 2) % 4, r // 8
    y, zh = c % 4, c // 4

    def row_dev(x_, zl_, core_):
        return {"row": zl_ * 8 + x_ * 2 + core_, "col": c}

    def col_dev(y_, zh_):
        return {"row": r, "col": zh_ * 4 + y_}

    twin = row_dev(x, zl, 1 - core)
    x_up, x_dn = row_dev((x + 1) % 4, zl, core), row_dev((x + 3) % 4, zl, core)
    z_pair = row_dev(x, 1 - zl, core)
    y_up, y_dn = col_dev((y + 1) % 4, zh), col_dev((y + 3) % 4, zh)

    x_far = row_dev((x + 2) % 4, zl, core)

    barrier = pltpu.get_barrier_semaphore()
    for dev in [twin, x_up, x_dn, z_pair, x_far, y_up, y_dn] + [col_dev(y, (zh + o) % 4) for o in (1, 2, 3)]:
        pl.semaphore_signal(barrier, inc=1, device_id=dev, device_id_type=MESH)
    pl.semaphore_wait(barrier, 10)

    def remote(src, dst, s, d, dev):
        return pltpu.make_async_remote_copy(
            src_ref=src, dst_ref=dst, send_sem=s, recv_sem=d, device_id=dev, device_id_type=MESH
        )

    own_act = pltpu.make_async_copy(act, slabs.at[r], local.at[0])
    own_grad = pltpu.make_async_copy(grad, gslabs.at[zh, y], local.at[1])
    own_act.start()
    own_grad.start()
    own_ob = pltpu.make_async_copy(obasis, obas, local.at[2])
    own_ob.start()

    def basis_copy(j):
        return pltpu.make_async_copy(
            basis.at[:, pl.ds(pl.multiple_of(j * WIDE, WIDE), WIDE)], bas.at[j], local.at[3 + j]
        )

    def slab_at(x_, zl_, core_):
        return slabs.at[zl_ * 8 + x_ * 2 + core_]

    LO, HI = slice(0, CIN // 2), slice(CIN // 2, CIN)

    def ship(n, src, dst, dev):
        d = remote(src, dst, asend.at[0], arecv.at[n], dev)
        d.start()

    def landed(n, dst, dev):
        remote(dst, dst, asend.at[0], arecv.at[n], dev).wait_recv()

    xm, xp, xo, zo = (x + 3) % 4, (x + 1) % 4, (x + 2) % 4, 1 - zl
    mine = slabs.at[r]

    ship(0, act, mine, z_pair)
    ship(1, act, mine, x_up)
    ship(2, act, mine, x_dn)
    ship(9, act, mine, twin)

    def gship(n, src, dst, dev):
        remote(src, dst, gsend.at[n], grecv.at[n], dev).start()

    def glanded(n, dst, dev):
        remote(dst, dst, gsend.at[n], grecv.at[n], dev).wait_recv()

    for j in range(STEPS):
        basis_copy(j).start()

    landed(0, slab_at(x, zo, core), z_pair)
    ship(3, slab_at(x, zo, core), slab_at(x, zo, core), x_up)
    ship(4, slab_at(x, zo, core), slab_at(x, zo, core), x_dn)
    ship(10, slab_at(x, zo, core), slab_at(x, zo, core), twin)

    for o in (1, 2, 3):
        h = (zh + o) % 4
        remote(grad, gslabs.at[zh, y], gsend.at[0], grecv.at[0], col_dev(y, h)).start()

    below, above, far = slab_at(xm, zl, core), slab_at(xp, zl, core), slab_at(xo, zl, core)
    landed(1, below, x_dn)
    ship(5, below.at[:, LO], below.at[:, LO], x_up)
    ship(11, below, below, twin)
    landed(2, above, x_up)
    ship(6, above.at[:, HI], above.at[:, HI], x_dn)
    ship(12, above, above, twin)

    order = ((x, zl), (x, zo), (xm, zl), (xp, zl), (xo, zl), (xm, zo), (xp, zo), (xo, zo))

    def join(i):
        k = order[i][1] * 4 + order[i][0]
        a = slabs[2 * k].astype(F32)
        b = slabs[2 * k + 1].astype(F32)
        acts[pl.ds(i * 144, 144), :] = jnp.concatenate([a, b], axis=0).astype(BF)

    own_act.wait()
    for n, i in ((9, 0), (10, 1), (11, 2), (12, 3)):
        landed(n, slab_at(*order[i], 1 - core), twin)
        join(i)

    def act_far():
        landed(5, far.at[:, LO], x_dn)
        landed(6, far.at[:, HI], x_up)
        ship(7, far, far, z_pair)
        ship(15, far, far, twin)

    def act_cross():
        for n, x_, dev, out_n in ((3, xm, x_dn, 13), (4, xp, x_up, 14)):
            landed(n, slab_at(x_, zo, core), dev)
            ship(out_n, slab_at(x_, zo, core), slab_at(x_, zo, core), twin)

    def act_last():
        landed(7, slab_at(xo, zo, core), z_pair)
        ship(16, slab_at(xo, zo, core), slab_at(xo, zo, core), twin)
        for n, i in ((15, 4), (13, 5), (14, 6), (16, 7)):
            landed(n, slab_at(*order[i], 1 - core), twin)
            join(i)

    label = ids[...].reshape(1, TOK)
    weights = [
        1.0 / (jnp.sum((label == s).astype(F32), axis=1, keepdims=True) * NSEQ) for s in range(NSEQ)
    ]
    labels[...] = jnp.broadcast_to(label.astype(F32), (128, TOK)).T

    up, dn, op = (y + 1) % 4, (y + 3) % 4, (y + 2) % 4
    others = [(zh + o) % 4 for o in (1, 2, 3)]

    def msg(j, m, n_send, n_recv, src, dst, dev):
        return remote(src, dst, send.at[n_send], recv.at[j, m, n_recv], dev)

    def lanes(m):
        return pl.ds(*LANES[m])

    def stage_compute(j, m):
        ln = lanes(m)
        if m == 0:
            basis_copy(j).wait()
        prod = jnp.dot(acts[ln, :], bas[j], preferred_element_type=F32)
        part[j, :, :, ln] = prod.T.reshape(4, QUARTER, LANES[m][1])
        half_out[j, 0, :, ln] = part[j, op, :HALF, ln].astype(BF)
        half_out[j, 1, :, ln] = part[j, op, HALF:, ln].astype(BF)
        for n, dev in ((0, y_up), (1, y_dn)):
            msg(j, m, 0, n, half_out.at[j, n, :, ln], half_in.at[j, n, :, ln], dev).start()

    def stage_half(j, m):
        ln = lanes(m)
        msg(j, m, 0, 0, half_out.at[j, 0, :, ln], half_in.at[j, 0, :, ln], y_dn).wait_recv()
        full_out[j, 0, :HALF, ln] = (part[j, up, :HALF, ln] + half_in[j, 0, :, ln].astype(F32)).astype(BF)
        full_out[j, 0, HALF:, ln] = part[j, up, HALF:, ln].astype(BF)
        msg(j, m, 1, 2, full_out.at[j, 0, :, ln], full_in.at[j, 0, :, ln], y_up).start()
        msg(j, m, 0, 1, half_out.at[j, 1, :, ln], half_in.at[j, 1, :, ln], y_up).wait_recv()
        full_out[j, 1, HALF:, ln] = (part[j, dn, HALF:, ln] + half_in[j, 1, :, ln].astype(F32)).astype(BF)
        full_out[j, 1, :HALF, ln] = part[j, dn, :HALF, ln].astype(BF)
        msg(j, m, 1, 2, full_out.at[j, 1, :, ln], full_in.at[j, 1, :, ln], y_dn).start()

    def stage_full(j, m):
        ln = lanes(m)
        msg(j, m, 1, 2, full_out.at[j, :, :, ln], full_in.at[j, :, :, ln], y_dn).wait_recv()
        total = part[j, y, :, ln] + full_in[j, 0, :, ln].astype(F32) + full_in[j, 1, :, ln].astype(F32)
        part[j, y, :, ln] = total
        z_out[j, :, :, ln] = total.astype(BF).reshape(4, PIECE, LANES[m][1])
        for h in others:
            msg(j, m, 2, 3, z_out.at[j, h, :, ln], z_in.at[j, zh, :, ln], col_dev(y, h)).start()

    def stage_z(j, m):
        ln = lanes(m)
        total = part[j, y, pl.ds(pl.multiple_of(zh * PIECE, PIECE), PIECE), ln]
        msg(j, m, 2, 3, z_out.at[j, 0:3, :, ln], z_in.at[j, 0:3, :, ln], y_up).wait_recv()
        for h in others:
            total = total + z_in[j, h, :, ln].astype(F32)
        rot[j, y, zh, :, ln] = total.astype(BF)
        piece = rot.at[j, y, zh, :, ln]
        for h in others:
            msg(j, m, 3, 4, piece, piece, col_dev(y, h)).start()

    def stage_gather(j, m):
        ln = lanes(m)
        pieces = rot.at[j, y, 0:3, :, ln]
        msg(j, m, 3, 4, pieces, pieces, y_up).wait_recv()
        quarter = rot.at[j, y, :, :, ln]
        msg(j, m, 4, 5, quarter, quarter, y_up).start()
        msg(j, m, 4, 6, quarter, quarter, y_dn).start()

    def stage_relay(j, m):
        ln = lanes(m)
        below, above = rot.at[j, dn, :, :, ln], rot.at[j, up, :, :, ln]
        msg(j, m, 4, 5, below, below, y_dn).wait_recv()
        piece = rot.at[j, dn, 0:2, :, ln]
        msg(j, m, 5, 7, piece, piece, y_up).start()
        msg(j, m, 4, 6, above, above, y_up).wait_recv()
        piece = rot.at[j, up, 2:4, :, ln]
        msg(j, m, 5, 7, piece, piece, y_dn).start()

    def stage_last(j, m):
        ln = lanes(m)
        quarter = rot.at[j, op, :, :, ln]
        msg(j, m, 5, 7, quarter, quarter, y_dn).wait_recv()

    def out_copy(j):
        return pltpu.make_async_copy(
            res.at[j], out.at[pl.ds(pl.multiple_of(j * WIDE, WIDE), WIDE), :], local.at[10 + j]
        )

    def square(j):
        a = rot[j].reshape(WIDE, TOK)
        for h in range(2):
            total = None
            for s in range(NSEQ):
                p = jnp.dot(a, gmask[s, h], preferred_element_type=F32)
                term = p * p * weights[s]
                total = term if total is None else total + term
            res[j, :, pl.ds(h * 256, 256)] = total
        out_copy(j).start()

    def grad_y():
        own_grad.wait()
        remote(gslabs.at[0:3, 0], gslabs.at[0:3, 0], gsend.at[0], grecv.at[0], y_up).wait_recv()
        mine_y = gslabs.at[:, y]
        remote(mine_y, mine_y, gsend.at[0], grecv.at[1], y_up).start()
        remote(mine_y, mine_y, gsend.at[0], grecv.at[2], y_dn).start()

    def grad_relay():
        below_y, above_y = gslabs.at[:, dn], gslabs.at[:, up]
        remote(below_y, below_y, gsend.at[0], grecv.at[1], y_dn).wait_recv()
        piece = gslabs.at[0:2, dn]
        remote(piece, piece, gsend.at[0], grecv.at[3], y_up).start()
        remote(above_y, above_y, gsend.at[0], grecv.at[2], y_up).wait_recv()
        piece = gslabs.at[2:4, up]
        remote(piece, piece, gsend.at[0], grecv.at[3], y_dn).start()

    def grad_rotate():
        remote(gslabs.at[:, op], gslabs.at[:, op], gsend.at[0], grecv.at[3], y_up).wait_recv()
        own_ob.wait()

        def rotate(k, carry):
            a = gslabs[k // 2, 2 * (k % 2)].astype(F32)
            b = gslabs[k // 2, 2 * (k % 2) + 1].astype(F32)
            both = jnp.concatenate([a, b], axis=0).astype(BF)
            prod = jnp.dot(both, obas[...], preferred_element_type=F32)
            gpart[0, k] = prod[:, :256]
            gpart[1, k] = prod[:, 256:]
            return carry

        lax.fori_loop(0, 8, rotate, 0)
        gship(16, gpart.at[1 - core], gcore, twin)

    def x_dev(x_):
        return row_dev(x_, zl, core)

    def grad_core():
        glanded(16, gcore, twin)

        def add(k, carry):
            gpart[core, k] = gpart[core, k] + gcore[k]
            return carry

        lax.fori_loop(0, 8, add, 0)
        for o in (1, 2, 3):
            k = (x + o) % 4
            pair = gpart.at[core, pl.ds(2 * k, 2)]
            remote(pair, gin.at[x], gsend.at[17], grecv.at[17], x_dev(k)).start()

    def grad_x():
        glanded(17, gin.at[0:3], x_up)
        for o in (1, 2, 3):
            k = (x + o) % 4
            for i in range(2):
                gpart[core, 2 * x + i] = gpart[core, 2 * x + i] + gin[k, i]
        gship(21, gpart.at[core, 2 * x + zo], gpair, z_pair)

    def grad_sum():
        glanded(21, gpair, z_pair)
        grot[core, 2 * x + zl] = (gpart[core, 2 * x + zl] + gpair[...]).astype(BF)
        piece = grot.at[core, 2 * x + zl]
        gship(22, piece, piece, z_pair)

    def grad_z():
        glanded(22, grot.at[core, 2 * x + zo], z_pair)
        pair = grot.at[core, pl.ds(2 * x, 2)]
        for o in (1, 2, 3):
            k = (x + o) % 4
            remote(pair, pair, gsend.at[23], grecv.at[23], x_dev(k)).start()

    def grad_gather():
        glanded(23, grot.at[core, 0:6], x_up)
        gship(27, grot.at[core], grot.at[core], twin)

    def grad_done():
        glanded(27, grot.at[1 - core], twin)
        for i in range(8):
            k = order[i][1] * 4 + order[i][0]
            rows = labels[pl.ds(pl.multiple_of(k * 144, 16), 144), :]
            for s in range(NSEQ):
                member = (rows == s).astype(F32).astype(BF)
                member = jnp.concatenate([member, member], axis=1)
                for h in range(2):
                    gmask[s, h, pl.ds(i * 144, 144), :] = grot[h, k] * member
        lax.fori_loop(0, (GDONE - LAGS[-1]) // 2 - LEAD, lambda j, carry: (square(j), carry)[1], 0)

    stages = [stage_compute, stage_half, stage_full, stage_z, stage_gather, stage_relay, stage_last]
    deep = LAGS[-1]
    extras = {
        0: act_far, 1: grad_y, 2: act_cross, 4: act_last, 5: grad_relay, 8: grad_rotate, 9: grad_core,
        16: grad_x, 18: grad_sum, 20: grad_z, 24: grad_gather, GDONE: grad_done,
    }

    def turn(pair, carry):
        for parity in range(2):
            now = 2 * pair + parity
            for lag, stage in zip(LAGS, stages):
                m = (parity + lag) % 2
                j = (now - lag - m) // 2 - m * LEAD

                @pl.when((j >= 0) & (j < STEPS))
                def _():
                    stage(j, m)
                    if lag == deep and m == 1:
                        pl.when(now >= GDONE)(lambda: square(j))

            for at, extra in extras.items():
                if at % 2 == parity:
                    pl.when(now == at)(extra)

        return carry

    lax.fori_loop(0, (2 * (STEPS - 1 + LEAD) + 1 + deep) // 2 + 1, turn, 0)

    for j in range(STEPS):
        out_copy(j).wait()

    def sent(sem, ref):
        remote(ref, ref, sem, sem, twin).wait_send()

    sent(send.at[0], half_out)
    sent(send.at[1], full_out)
    sent(send.at[2], z_out.at[:, 0:3])
    sent(send.at[3], z_out.at[:, 0:3])
    sent(send.at[4], rot.at[:, 0:2])
    sent(send.at[5], rot.at[:, 0])
    sent(asend.at[0], slabs.at[0:15])
    sent(gsend.at[0], gslabs.at[0:3])
    sent(gsend.at[0], gslabs.at[0, 0:3])
    sent(gsend.at[16], gcore)
    sent(gsend.at[17], gin.at[0:3])
    sent(gsend.at[21], gpair)
    sent(gsend.at[22], grot.at[core, 0])
    sent(gsend.at[23], grot.at[core, 0:6])
    sent(gsend.at[27], grot.at[core])


def shards(activations, grad_outputs, input_basis, output_basis, segment_ids):
    hbm = pl.BlockSpec(memory_space=pl.ANY)
    dma = pltpu.SemaphoreType.DMA
    return pl.pallas_call(
        kernel,
        out_shape=jax.ShapeDtypeStruct((CIN, GIN), F32),
        in_specs=[hbm, hbm, hbm, hbm, pl.BlockSpec(memory_space=pltpu.VMEM)],
        out_specs=hbm,
        scratch_shapes=[
            pltpu.VMEM((16, SLAB, CIN), BF),
            pltpu.VMEM((TOK, CIN), BF),
            pltpu.VMEM((STEPS, CIN, WIDE), BF),
            pltpu.VMEM((GIN, GIN), BF),
            pltpu.VMEM((STEPS, 4, QUARTER, TOK), F32),
            pltpu.VMEM((STEPS, 2, HALF, TOK), BF),
            pltpu.VMEM((STEPS, 2, HALF, TOK), BF),
            pltpu.VMEM((STEPS, 2, QUARTER, TOK), BF),
            pltpu.VMEM((STEPS, 2, QUARTER, TOK), BF),
            pltpu.VMEM((STEPS, 4, PIECE, TOK), BF),
            pltpu.VMEM((STEPS, 4, PIECE, TOK), BF),
            pltpu.VMEM((STEPS, 4, 4, PIECE, TOK), BF),
            pltpu.VMEM((STEPS, WIDE, GIN), F32),
            pltpu.VMEM((4, 4, SLAB, GIN), BF),
            pltpu.VMEM((2, 8, 144, 256), F32),
            pltpu.VMEM((8, 144, 256), F32),
            pltpu.VMEM((4, 2, 144, 256), F32),
            pltpu.VMEM((144, 256), F32),
            pltpu.VMEM((2, 8, 144, 256), BF),
            pltpu.VMEM((NSEQ, 2, TOK, 256), BF),
            pltpu.VMEM((TOK, 128), F32),
            dma((6,)),
            dma((STEPS, 2, 8)),
            dma((1,)),
            dma((17,)),
            dma((28,)),
            dma((28,)),
            dma((17,)),
        ],
        compiler_params=pltpu.CompilerParams(
            collective_id=0, has_side_effects=True, vmem_limit_bytes=60 * 1024 * 1024
        ),
        cost_estimate=pl.CostEstimate(flops=15_000_000_000, bytes_accessed=16_000_000, transcendentals=0),
    )(activations, grad_outputs, input_basis, output_basis, segment_ids)


def solution(mesh):
    placed = (P("row", "col"), P("col", "row"), P("col", "row"), P("row", "col"), P())
    return jax.shard_map(
        shards, mesh=mesh, in_specs=placed, out_specs=P("row", "col"), check_vma=False
    )
```

time: 357 us -> 122 us (0.34)
  waiting for transfers between devices: 212 us -> 0 us
  Pallas kernels: 0 us -> 116 us
  blocking collectives: 92.7 us -> 0 us
  matrix products: 27.3 us -> 0 us
  between operations: 19.1 us -> 0.01 us
    reduce_scatter x1 -> x0, waiting for transfers between devices: 118 us -> none  [shards(): lax.psum_scatter(lax.dot_general(input_basis, act_all, (((0,), (1,)), (()...]
    pallas_call x0 -> x1, Pallas kernels: none -> 116 us  [shards(): pl.pallas_call(kernel, out_shape=jax.ShapeDtypeStruct((CIN, GIN), F32), i...]
    psum x1 -> x0, blocking collectives: 92.7 us -> none  [shards(): grad_rot = lax.psum(grad_part, 'row').astype(jnp.bfloat16)]
    all_gather x3 -> x0, waiting for transfers between devices: 92.2 us -> none  [the longest x1 46.2 us: shards(): grad_all = lax.all_gather(grad_outputs, 'col', axis=0, tiled=True)]
    dot_general x5 -> x0, matrix products: 27.3 us -> none  [the longest x1 13.8 us: shards(): lax.dot_general(input_basis, act_all, (((0,), (1,)), ((), ())), preferred...]
    unnamed x8 -> x1, local copies, waits for them, and re-layouts: 0.02 us -> 4.25 us
  transfers between devices with their start and end apart: 4 -> 0, of which waited for: 3 -> 0; matrix products, arithmetic and copies ran while one was open for 2% -> 0% of each run, Pallas kernels for 0% -> 0%
where the time goes in v2:
time: 122 us; the launch traced here: 121 us
  Pallas kernels  116 us (95%)
  local copies, waits for them, and re-layouts  4.25 us (3%)
    pallas_call x1, Pallas kernels, shards(): pl.pallas_call(kernel, out_shape=jax.ShapeDtypeStruct((CIN, GIN), F32), i...  116 us
    unnamed x1, local copies, waits for them, and re-layouts  4.25 us

profile of v2, /device:TPU:1, one launch (start us, length us, event | category | flops | bytes accessed | tf_op | source)
XLA Modules:
  0.0 120.6 jit_solution(5116148072653970482)
XLA Ops:
  0.0 116.4 %shard_map.55 = f32[1792,512]{1,0:T(8,128)} custom-call(bf16[72,1792]{1,0:T(8,128)(2,1)} %act.1, bf16[72,512]{1,0:T(8,128)(2,1)} %grad.1, bf16[1792,1792]{1,0:T(8,128)(2,1)} %basis.1, bf16[512,512]{1,0:T(8,128)(2,1)} %obasis.1, s32[1152]{0:T(1024)} %ids.1), custom_call_target="tpu_custom_call" | custom-call | flops 15000000512 | bytes 16000000 | tf_op jit(solution)/shard_map/pallas_call | solution.py:384
  116.4 4.2 %copy.7 = f32[1792,512]{1,0:T(8,128)} copy(f32[1792,512]{1,0:T(8,128)} %shard_map.55) | data formatting | bytes 7340032

commit v3 on v2

--- a/solution.py
+++ b/solution.py
@@ -18,7 +18,7 @@
 PIECE = 16
 LANES = ((0, 512), (512, 640))
 LEAD = 2
-GDONE = 26
+GDONE = 28
 LAGS = (0, 2, 4, 7, 10, 12, 14)
 BF = jnp.bfloat16
 F32 = jnp.float32
@@ -98,15 +98,6 @@
     for j in range(STEPS):
         basis_copy(j).start()
 
-    landed(0, slab_at(x, zo, core), z_pair)
-    ship(3, slab_at(x, zo, core), slab_at(x, zo, core), x_up)
-    ship(4, slab_at(x, zo, core), slab_at(x, zo, core), x_dn)
-    ship(10, slab_at(x, zo, core), slab_at(x, zo, core), twin)
-
-    for o in (1, 2, 3):
-        h = (zh + o) % 4
-        remote(grad, gslabs.at[zh, y], gsend.at[0], grecv.at[0], col_dev(y, h)).start()
-
     below, above, far = slab_at(xm, zl, core), slab_at(xp, zl, core), slab_at(xo, zl, core)
     landed(1, below, x_dn)
     ship(5, below.at[:, LO], below.at[:, LO], x_up)
@@ -114,6 +105,15 @@
     landed(2, above, x_up)
     ship(6, above.at[:, HI], above.at[:, HI], x_dn)
     ship(12, above, above, twin)
+
+    landed(0, slab_at(x, zo, core), z_pair)
+    ship(3, slab_at(x, zo, core), slab_at(x, zo, core), x_up)
+    ship(4, slab_at(x, zo, core), slab_at(x, zo, core), x_dn)
+    ship(10, slab_at(x, zo, core), slab_at(x, zo, core), twin)
+
+    for o in (1, 2, 3):
+        h = (zh + o) % 4
+        remote(grad, gslabs.at[zh, y], gsend.at[0], grecv.at[0], col_dev(y, h)).start()
 
     order = ((x, zl), (x, zo), (xm, zl), (xp, zl), (xo, zl), (xm, zo), (xp, zo), (xo, zo))
 
@@ -329,10 +329,9 @@
 
     stages = [stage_compute, stage_half, stage_full, stage_z, stage_gather, stage_relay, stage_last]
     deep = LAGS[-1]
-    extras = {
-        0: act_far, 1: grad_y, 2: act_cross, 4: act_last, 5: grad_relay, 8: grad_rotate, 9: grad_core,
-        16: grad_x, 18: grad_sum, 20: grad_z, 24: grad_gather, GDONE: grad_done,
-    }
+    extras = (
+        (1, act_far), (3, grad_y), (4, act_cross), (4, act_last), (7, grad_relay), (10, grad_rotate), (11, grad_core), (18, grad_x), (20, grad_sum), (22, grad_z), (25, grad_gather), (GDONE, grad_done),
+    )
 
     def turn(pair, carry):
         for parity in range(2):
@@ -347,7 +346,7 @@
                     if lag == deep and m == 1:
                         pl.when(now >= GDONE)(lambda: square(j))
 
-            for at, extra in extras.items():
+            for at, extra in extras:
                 if at % 2 == parity:
                     pl.when(now == at)(extra)
 

time: 122 us -> 117 us (0.959); the launches traced: 121 us -> 117 us
  Pallas kernels: 116 us -> 113 us
    pallas_call x1, Pallas kernels: 116 us -> 113 us  [shards(): pl.pallas_call(kernel, out_shape=jax.ShapeDtypeStruct((CIN, GIN), F32), i...]
where the time goes in v3:
time: 117 us
  Pallas kernels  113 us (97%)
  local copies, waits for them, and re-layouts  4.25 us (4%)
    pallas_call x1, Pallas kernels, shards(): pl.pallas_call(kernel, out_shape=jax.ShapeDtypeStruct((CIN, GIN), F32), i...  113 us
    unnamed x1, local copies, waits for them, and re-layouts  4.25 us

profile of v3, /device:TPU:1, one launch (start us, length us, event | category | flops | bytes accessed | tf_op | source)
XLA Modules:
  0.0 117.3 jit_solution(16211055084952684205)
XLA Ops:
  0.0 113.0 %shard_map.55 = f32[1792,512]{1,0:T(8,128)} custom-call(bf16[72,1792]{1,0:T(8,128)(2,1)} %act.1, bf16[72,512]{1,0:T(8,128)(2,1)} %grad.1, bf16[1792,1792]{1,0:T(8,128)(2,1)} %basis.1, bf16[512,512]{1,0:T(8,128)(2,1)} %obasis.1, s32[1152]{0:T(1024)} %ids.1), custom_call_target="tpu_custom_call" | custom-call | flops 15000000512 | bytes 16000000 | tf_op jit(solution)/shard_map/pallas_call | solution.py:383
  113.0 4.2 %copy.7 = f32[1792,512]{1,0:T(8,128)} copy(f32[1792,512]{1,0:T(8,128)} %shard_map.55) | data formatting | bytes 7340032

commit v4 on v3

--- a/solution.py
+++ b/solution.py
@@ -17,9 +17,9 @@
 HALF = 32
 PIECE = 16
 LANES = ((0, 512), (512, 640))
-LEAD = 2
-GDONE = 28
-LAGS = (0, 2, 4, 7, 10, 12, 14)
+LEAD = 1
+GDONE = 24
+LAGS = ((0, 2, 4, 6, 8, 10, 12), (0, 2, 4, 6, 8, 10, 12))
 BF = jnp.bfloat16
 F32 = jnp.float32
 
@@ -85,8 +85,10 @@
     mine = slabs.at[r]
 
     ship(0, act, mine, z_pair)
-    ship(1, act, mine, x_up)
-    ship(2, act, mine, x_dn)
+    ship(1, act.at[:, LO], mine.at[:, LO], x_up)
+    ship(2, act.at[:, HI], mine.at[:, HI], x_dn)
+    ship(17, act.at[:, HI], mine.at[:, HI], x_up)
+    ship(18, act.at[:, LO], mine.at[:, LO], x_dn)
     ship(9, act, mine, twin)
 
     def gship(n, src, dst, dev):
@@ -99,11 +101,13 @@
         basis_copy(j).start()
 
     below, above, far = slab_at(xm, zl, core), slab_at(xp, zl, core), slab_at(xo, zl, core)
-    landed(1, below, x_dn)
+    landed(1, below.at[:, LO], x_dn)
     ship(5, below.at[:, LO], below.at[:, LO], x_up)
+    landed(2, above.at[:, HI], x_up)
+    ship(6, above.at[:, HI], above.at[:, HI], x_dn)
+    landed(17, below.at[:, HI], x_dn)
     ship(11, below, below, twin)
-    landed(2, above, x_up)
-    ship(6, above.at[:, HI], above.at[:, HI], x_dn)
+    landed(18, above.at[:, LO], x_up)
     ship(12, above, above, twin)
 
     landed(0, slab_at(x, zo, core), z_pair)
@@ -325,26 +329,29 @@
                 member = jnp.concatenate([member, member], axis=1)
                 for h in range(2):
                     gmask[s, h, pl.ds(i * 144, 144), :] = grot[h, k] * member
-        lax.fori_loop(0, (GDONE - LAGS[-1]) // 2 - LEAD, lambda j, carry: (square(j), carry)[1], 0)
+        lax.fori_loop(0, (GDONE - LAGS[1][-1]) // 2 - LEAD, lambda j, carry: (square(j), carry)[1], 0)
 
     stages = [stage_compute, stage_half, stage_full, stage_z, stage_gather, stage_relay, stage_last]
-    deep = LAGS[-1]
+    deep = LAGS[1][-1]
     extras = (
-        (1, act_far), (3, grad_y), (4, act_cross), (4, act_last), (7, grad_relay), (10, grad_rotate), (11, grad_core), (18, grad_x), (20, grad_sum), (22, grad_z), (25, grad_gather), (GDONE, grad_done),
+        (0, act_far), (2, grad_y), (2, act_cross), (2, act_last), (5, grad_relay), (8, grad_rotate), (9, grad_core), (14, grad_x), (16, grad_sum), (18, grad_z), (21, grad_gather), (GDONE, grad_done),
     )
 
     def turn(pair, carry):
         for parity in range(2):
             now = 2 * pair + parity
-            for lag, stage in zip(LAGS, stages):
-                m = (parity + lag) % 2
-                j = (now - lag - m) // 2 - m * LEAD
-
-                @pl.when((j >= 0) & (j < STEPS))
-                def _():
-                    stage(j, m)
-                    if lag == deep and m == 1:
-                        pl.when(now >= GDONE)(lambda: square(j))
+            for k, stage in enumerate(stages):
+                for m in range(2):
+                    lag = LAGS[m][k]
+                    if (parity + lag + m) % 2:
+                        continue
+                    j = (now - lag - m) // 2 - m * LEAD
+
+                    @pl.when((j >= 0) & (j < STEPS))
+                    def _():
+                        stage(j, m)
+                        if k == len(stages) - 1 and m == 1:
+                            pl.when(now >= GDONE)(lambda: square(j))
 
             for at, extra in extras:
                 if at % 2 == parity:
@@ -410,7 +417,7 @@
             dma((6,)),
             dma((STEPS, 2, 8)),
             dma((1,)),
-            dma((17,)),
+            dma((19,)),
             dma((28,)),
             dma((28,)),
             dma((17,)),

time: 117 us -> 117 us (level)
  no operation moved by 1% of the time
where the time goes in v4:
time: 117 us
  Pallas kernels  113 us (97%)
  local copies, waits for them, and re-layouts  4.25 us (4%)
    pallas_call x1, Pallas kernels, shards(): pl.pallas_call(kernel, out_shape=jax.ShapeDtypeStruct((CIN, GIN), F32), i...  113 us
    unnamed x1, local copies, waits for them, and re-layouts  4.25 us

profile of v4, /device:TPU:1, one launch (start us, length us, event | category | flops | bytes accessed | tf_op | source)
XLA Modules:
  0.0 116.8 jit_solution(11581911279211287790)
XLA Ops:
  0.0 112.6 %shard_map.55 = f32[1792,512]{1,0:T(8,128)} custom-call(bf16[72,1792]{1,0:T(8,128)(2,1)} %act.1, bf16[72,512]{1,0:T(8,128)(2,1)} %grad.1, bf16[1792,1792]{1,0:T(8,128)(2,1)} %basis.1, bf16[512,512]{1,0:T(8,128)(2,1)} %obasis.1, s32[1152]{0:T(1024)} %ids.1), custom_call_target="tpu_custom_call" | custom-call | flops 15000000512 | bytes 16000000 | tf_op jit(solution)/shard_map/pallas_call | solution.py:390
  112.6 4.2 %copy.7 = f32[1792,512]{1,0:T(8,128)} copy(f32[1792,512]{1,0:T(8,128)} %shard_map.55) | data formatting | bytes 7340032

commit v5 on v4

--- a/solution.py
+++ b/solution.py
@@ -329,12 +329,15 @@
                 member = jnp.concatenate([member, member], axis=1)
                 for h in range(2):
                     gmask[s, h, pl.ds(i * 144, 144), :] = grot[h, k] * member
-        lax.fori_loop(0, (GDONE - LAGS[1][-1]) // 2 - LEAD, lambda j, carry: (square(j), carry)[1], 0)
+        lax.fori_loop(0, 2, lambda j, carry: (square(j), carry)[1], 0)
+
+    def late_squares():
+        lax.fori_loop(2, (GDONE - LAGS[1][-1]) // 2 - LEAD, lambda j, carry: (square(j), carry)[1], 0)
 
     stages = [stage_compute, stage_half, stage_full, stage_z, stage_gather, stage_relay, stage_last]
     deep = LAGS[1][-1]
     extras = (
-        (0, act_far), (2, grad_y), (2, act_cross), (2, act_last), (5, grad_relay), (8, grad_rotate), (9, grad_core), (14, grad_x), (16, grad_sum), (18, grad_z), (21, grad_gather), (GDONE, grad_done),
+        (0, act_far), (2, grad_y), (2, act_cross), (2, act_last), (5, grad_relay), (8, grad_rotate), (9, grad_core), (14, grad_x), (16, grad_sum), (18, grad_z), (21, grad_gather), (GDONE, grad_done), (GDONE + 2, late_squares),
     )
 
     def turn(pair, carry):

time: 117 us -> 116 us (level)
  no operation moved by 1% of the time
where the time goes in v5:
time: 116 us
  Pallas kernels  112 us (97%)
  local copies, waits for them, and re-layouts  4.25 us (4%)
    pallas_call x1, Pallas kernels, shards(): pl.pallas_call(kernel, out_shape=jax.ShapeDtypeStruct((CIN, GIN), F32), i...  112 us
    unnamed x1, local copies, waits for them, and re-layouts  4.25 us

profile of v5, /device:TPU:1, one launch (start us, length us, event | category | flops | bytes accessed | tf_op | source)
XLA Modules:
  0.0 116.2 jit_solution(15819707975909118939)
XLA Ops:
  0.0 111.9 %shard_map.55 = f32[1792,512]{1,0:T(8,128)} custom-call(bf16[72,1792]{1,0:T(8,128)(2,1)} %act.1, bf16[72,512]{1,0:T(8,128)(2,1)} %grad.1, bf16[1792,1792]{1,0:T(8,128)(2,1)} %basis.1, bf16[512,512]{1,0:T(8,128)(2,1)} %obasis.1, s32[1152]{0:T(1024)} %ids.1), custom_call_target="tpu_custom_call" | custom-call | flops 15000000512 | bytes 16000000 | tf_op jit(solution)/shard_map/pallas_call | solution.py:393
  112.0 4.2 %copy.7 = f32[1792,512]{1,0:T(8,128)} copy(f32[1792,512]{1,0:T(8,128)} %shard_map.55) | data formatting | bytes 7340032
